TPU v7x, 256 devices: a whole 4x4x8 slice. The times are simulated.
256 devices in a mesh: grp: 4 (over z_hi, core), cond: 16 (over z_lo, x), val: 4 (over y).
Axes of the slice: x: 4, y: 4, z: 8 (z_hi: 2, z_lo: 4; z = z_hi * 4 + z_lo), core: 2. Of those that a mesh axis runs over, the one named last changes fastest.
Arguments:
- screened: bfloat16 [8192, 8192], P('cond', ('grp', 'val')), may hold values from -0.0625 to 0.0625
- valence: bfloat16 [8192, 256], P(('grp', 'val')), may hold values from -6 to 6
- first_band: int32 [512], replicated, may hold values from 0 to 255
- second_band: int32 [512], replicated, may hold values from 0 to 255
- conduction: bfloat16 [512, 8192], P('cond'), may hold values from -6 to 6
- partners: int32 [4, 16, 4], P('grp', 'cond'), may hold values from -1 to 15, as said below
Outputs:
- kernel: float32 [4, 16, 4, 1024, 512], P('grp', 'cond', None, None, 'val')
Inputs may be any that keep to these rules, and one draw needn't show every extreme that they name: partners[g, a, s] is -1 (empty slot) or a block b with a <= b; for every a, each b from a to 15 stands exactly once in partners[:, a, :]; in conduction row 0 some groups fill all 4 slots.
All inputs are finite; a program needn't handle non-finite values.
Results may differ from a plain program's by a relative error of at most 0.0049.
Values may be sent and summed in bfloat16 or wider, within the bound.
A program may use at most 64 MiB of HBM per device.

v0:
```python
import math

import jax
import jax.numpy as jnp
from jax import lax
from jax.sharding import PartitionSpec as P


def shifted(block, axis, distance):
    devices = range(lax.axis_size(axis))
    route = [(i - distance, i) for i in devices if i - distance in devices]
    return lax.ppermute(block, axis, route)


def pair_kernel(left_bands, right_bands, mixed):
    band_block = left_bands.shape[0]
    point_count = left_bands.shape[1]
    point_block = min(2048, point_count)
    total = jnp.zeros((band_block * band_block, mixed.shape[1]), jnp.float32)
    for offset in range(0, point_count, point_block):
        left_part = left_bands[:, offset : offset + point_block].astype(jnp.float32)
        right_part = right_bands[:, offset : offset + point_block].astype(jnp.float32)
        density = (
            (left_part[:, None, :] * right_part[None, :, :])
            .reshape(band_block * band_block, point_block)
            .astype(jnp.bfloat16)
        )
        total = total + jnp.dot(
            density, mixed[offset : offset + point_block], preferred_element_type=jnp.float32
        )
    return total * (1.0 / math.sqrt(point_count))


def on_device(screened, valence, first_band, second_band, conduction, partners):
    band_count = valence.shape[1]
    band_index = lax.broadcasted_iota(jnp.int32, (band_count, first_band.shape[0]), 0)
    first_cols = jnp.dot(
        valence,
        (band_index == first_band[None, :]).astype(jnp.bfloat16),
        preferred_element_type=jnp.float32,
    )
    second_cols = jnp.dot(
        valence,
        (band_index == second_band[None, :]).astype(jnp.bfloat16),
        preferred_element_type=jnp.float32,
    )
    pair_density = (first_cols * second_cols).astype(jnp.bfloat16)
    partial_mix = jnp.dot(screened, pair_density, preferred_element_type=jnp.float32)
    pair_width = first_band.shape[0] // lax.axis_size("val")
    summed = lax.psum(partial_mix, ("grp", "val"))
    own_mixed = lax.dynamic_slice_in_dim(summed, lax.axis_index("val") * pair_width, pair_width, 1)
    mixed = lax.all_gather(own_mixed.astype(jnp.bfloat16), "cond", axis=0, tiled=True)
    owned = partners.reshape(-1)
    slot_count = owned.shape[0]
    band_block = conduction.shape[0]
    row_block = lax.axis_index("cond")
    blank_slots = jnp.zeros((slot_count, band_block * band_block, pair_width), jnp.float32)

    def deposit(kernel, holding, partner):
        matches = owned == partner

        def compute(current):
            slot_index = jnp.argmax(matches.astype(jnp.int32))
            kernel_term = pair_kernel(conduction, holding, mixed)
            return lax.dynamic_update_slice(current, kernel_term[None], (slot_index, 0, 0))

        return lax.cond(jnp.any(matches), compute, lambda kept: kept, kernel)

    kernel = deposit(blank_slots, conduction, row_block)

    def advance(distance, carry):
        holding, kernel = carry
        holding = shifted(holding, "cond", -1)
        return (holding, deposit(kernel, holding, row_block + distance))

    unused_block, kernel = lax.fori_loop(1, lax.axis_size("cond"), advance, (conduction, kernel))
    return kernel.reshape((1, 1) + kernel.shape)


def solution(mesh):
    in_specs = (
        P("cond", ("grp", "val")),
        P(("grp", "val"), None),
        P(),
        P(),
        P("cond", None),
        P("grp", "cond", None),
    )
    out_specs = P("grp", "cond", None, None, "val")
    return jax.shard_map(
        on_device, mesh=mesh, in_specs=in_specs, out_specs=out_specs, check_vma=False
    )
```

profile of v0, /device:TPU:8, one launch (start us, length us, event | category | flops | bytes accessed | tf_op | source)
XLA Modules:
  0.0 615.5 jit_solution(1210363220829330757)
XLA Ops:
  6.6 1.4 fusion.21
  8.0 1.6 convolution_bitcast_fusion
  9.6 99.6 %all-reduce.1 = bf16[512,512]{0,1:T(8,128)(2,1)S(1)} all-reduce(f32[512,512]{0,1:T(8,128)S(1)} %convolution_bitcast_fusion), channel_id=1, replica_groups=mesh['grp'=4,'cond'=16,'val'=4] {'grp','val'}, use_global_device_ids=true, to_apply=%region_1.0 | all-reduce | flops 262144 | bytes 1572864 | tf_op jit(solution)/shard_map/psum | solution.py:50
  112.1 82.3 %all-gather.2.cloned.1.call-done = bf16[8192,128]{0,1:T(8,128)(2,1)} async-done(((bf16[512,128]{0,1:T(8,128)(2,1)}), bf16[8192,128]{0,1:T(8,128)(2,1)}) %all-gather.2.cloned.1.call-update) | async-done | bytes 2097168 | tf_op jit(solution)/shard_map/all_gather | solution.py:52
  194.4 1.5 conditional.2
  194.4 1.5 broadcast_in_dim.0
  195.9 4.1 copy.8
  200.0 408.6 %while.18 = (s32[]{:T(128)}, bf16[32,8192]{1,0:T(8,128)(2,1)S(1)}, f32[4,1024,128]{2,1,0:T(8,128)}, s32[]{:T(128)}, s32[4]{0:T(128)S(1)}, /*index=5*/bf16[32,819...) while((s32[]{:T(128)}, bf16[32,8192]{1,0:T(8,128)(2,1)S(1)}, f32[4,1024,128]{2,1,0:T(8,128)}, ...), condition=%wide.region_10.11_spmd, body=%wide.region_5.0_spmd.sunk | while | flops 2165309440 | bytes 47710472 | solution.py:76
  200.0 1.3 collective-permute-start
  202.7 36.8 %collective-permute-done = bf16[32,8192]{1,0:T(8,128)(2,1)S(1)} collective-permute-done((bf16[32,8192]{1,0:T(8,128)(2,1)S(1)}, bf16[32,8192]{1,0:T(8,128)(2,1)S(1)}, u32[]{:S(2)}, u32[]{:S(2)}) %collective-permute-start) | collective-permute-done | bytes 524320 | tf_op jit(solution)/shard_map/while/body/eval_jaxpr/ppermute | solution.py:12
  239.6 1.3 collective-permute-start
  242.4 37.0 %collective-permute-done = bf16[32,8192]{1,0:T(8,128)(2,1)S(1)} collective-permute-done((bf16[32,8192]{1,0:T(8,128)(2,1)S(1)}, bf16[32,8192]{1,0:T(8,128)(2,1)S(1)}, u32[]{:S(2)}, u32[]{:S(2)}) %collective-permute-start) | collective-permute-done | bytes 524320 | tf_op jit(solution)/shard_map/while/body/eval_jaxpr/ppermute | solution.py:12
  279.4 1.3 collective-permute-start
  282.1 12.6 %collective-permute-done = bf16[32,8192]{1,0:T(8,128)(2,1)S(1)} collective-permute-done((bf16[32,8192]{1,0:T(8,128)(2,1)S(1)}, bf16[32,8192]{1,0:T(8,128)(2,1)S(1)}, u32[]{:S(2)}, u32[]{:S(2)}) %collective-permute-start) | collective-permute-done | bytes 524320 | tf_op jit(solution)/shard_map/while/body/eval_jaxpr/ppermute | solution.py:12
  294.8 1.3 collective-permute-start
  297.5 8.4 %collective-permute-done = bf16[32,8192]{1,0:T(8,128)(2,1)S(1)} collective-permute-done((bf16[32,8192]{1,0:T(8,128)(2,1)S(1)}, bf16[32,8192]{1,0:T(8,128)(2,1)S(1)}, u32[]{:S(2)}, u32[]{:S(2)}) %collective-permute-start) | collective-permute-done | bytes 524320 | tf_op jit(solution)/shard_map/while/body/eval_jaxpr/ppermute | solution.py:12
  305.9 1.3 collective-permute-start
  308.6 21.8 %collective-permute-done = bf16[32,8192]{1,0:T(8,128)(2,1)S(1)} collective-permute-done((bf16[32,8192]{1,0:T(8,128)(2,1)S(1)}, bf16[32,8192]{1,0:T(8,128)(2,1)S(1)}, u32[]{:S(2)}, u32[]{:S(2)}) %collective-permute-start) | collective-permute-done | bytes 524320 | tf_op jit(solution)/shard_map/while/body/eval_jaxpr/ppermute | solution.py:12
  330.5 1.3 collective-permute-start
  333.2 12.8 %collective-permute-done = bf16[32,8192]{1,0:T(8,128)(2,1)S(1)} collective-permute-done((bf16[32,8192]{1,0:T(8,128)(2,1)S(1)}, bf16[32,8192]{1,0:T(8,128)(2,1)S(1)}, u32[]{:S(2)}, u32[]{:S(2)}) %collective-permute-start) | collective-permute-done | bytes 524320 | tf_op jit(solution)/shard_map/while/body/eval_jaxpr/ppermute | solution.py:12
  346.0 1.3 collective-permute-start
  348.8 22.9 %collective-permute-done = bf16[32,8192]{1,0:T(8,128)(2,1)S(1)} collective-permute-done((bf16[32,8192]{1,0:T(8,128)(2,1)S(1)}, bf16[32,8192]{1,0:T(8,128)(2,1)S(1)}, u32[]{:S(2)}, u32[]{:S(2)}) %collective-permute-start) | collective-permute-done | bytes 524320 | tf_op jit(solution)/shard_map/while/body/eval_jaxpr/ppermute | solution.py:12
  371.7 20.4 %conditional.4 = (f32[4,1024,128]{2,1,0:T(8,128)}) conditional(s32[]{:T(128)} %convert_element_type.143, f32[4,1024,128]{2,1,0:T(8,128)} %get-tuple-element.272, (bf16[32,8192]{1,0:T(8,128)(2,1)S(1)}, bf16[32,8192]{1,0:T(8,128)(2,1)S(1)}, bf16[8192,128]{1,0:T(8,128)(2,1)}, pred[4]{0:T(512)(128)(4,1)S(1)}, f32[4,1024,128]{2,1,0:T(8,128)}) %tuple.71), branch_computations={%region_7.7_spmd, %region_8.0_spmd} | conditional | flops 2165309440 | bytes 44564540 | solution.py:67
  371.9 1.1 multiply_convert_fusion.7
  373.0 2.3 fusion.14
  376.4 2.3 convolution_add_fusion.5
  379.8 2.3 convolution_add_fusion.4
  382.1 3.0 multiply_convert_fusion.4
  387.8 4.4 fusion.10
  392.2 1.3 collective-permute-start
  394.9 11.2 %collective-permute-done = bf16[32,8192]{1,0:T(8,128)(2,1)S(1)} collective-permute-done((bf16[32,8192]{1,0:T(8,128)(2,1)S(1)}, bf16[32,8192]{1,0:T(8,128)(2,1)S(1)}, u32[]{:S(2)}, u32[]{:S(2)}) %collective-permute-start) | collective-permute-done | bytes 524320 | tf_op jit(solution)/shard_map/while/body/eval_jaxpr/ppermute | solution.py:12
  406.1 1.3 collective-permute-start
  408.9 36.0 %collective-permute-done = bf16[32,8192]{1,0:T(8,128)(2,1)S(1)} collective-permute-done((bf16[32,8192]{1,0:T(8,128)(2,1)S(1)}, bf16[32,8192]{1,0:T(8,128)(2,1)S(1)}, u32[]{:S(2)}, u32[]{:S(2)}) %collective-permute-start) | collective-permute-done | bytes 524320 | tf_op jit(solution)/shard_map/while/body/eval_jaxpr/ppermute | solution.py:12
  444.9 20.4 %conditional.4 = (f32[4,1024,128]{2,1,0:T(8,128)}) conditional(s32[]{:T(128)} %convert_element_type.143, f32[4,1024,128]{2,1,0:T(8,128)} %get-tuple-element.272, (bf16[32,8192]{1,0:T(8,128)(2,1)S(1)}, bf16[32,8192]{1,0:T(8,128)(2,1)S(1)}, bf16[8192,128]{1,0:T(8,128)(2,1)}, pred[4]{0:T(512)(128)(4,1)S(1)}, f32[4,1024,128]{2,1,0:T(8,128)}) %tuple.71), branch_computations={%region_7.7_spmd, %region_8.0_spmd} | conditional | flops 2165309440 | bytes 44564540 | solution.py:67
  445.2 1.1 multiply_convert_fusion.7
  446.2 2.3 fusion.14
  449.6 2.3 convolution_add_fusion.5
  453.0 2.3 convolution_add_fusion.4
  455.4 3.0 multiply_convert_fusion.4
  461.0 4.4 fusion.10
  465.4 1.3 collective-permute-start
  468.1 13.2 %collective-permute-done = bf16[32,8192]{1,0:T(8,128)(2,1)S(1)} collective-permute-done((bf16[32,8192]{1,0:T(8,128)(2,1)S(1)}, bf16[32,8192]{1,0:T(8,128)(2,1)S(1)}, u32[]{:S(2)}, u32[]{:S(2)}) %collective-permute-start) | collective-permute-done | bytes 524320 | tf_op jit(solution)/shard_map/while/body/eval_jaxpr/ppermute | solution.py:12
  481.3 20.4 %conditional.4 = (f32[4,1024,128]{2,1,0:T(8,128)}) conditional(s32[]{:T(128)} %convert_element_type.143, f32[4,1024,128]{2,1,0:T(8,128)} %get-tuple-element.272, (bf16[32,8192]{1,0:T(8,128)(2,1)S(1)}, bf16[32,8192]{1,0:T(8,128)(2,1)S(1)}, bf16[8192,128]{1,0:T(8,128)(2,1)}, pred[4]{0:T(512)(128)(4,1)S(1)}, f32[4,1024,128]{2,1,0:T(8,128)}) %tuple.71), branch_computations={%region_7.7_spmd, %region_8.0_spmd} | conditional | flops 2165309440 | bytes 44564540 | solution.py:67
  482.6 2.3 fusion.14
  486.0 2.3 convolution_add_fusion.5
  489.4 2.3 convolution_add_fusion.4
  491.8 3.0 multiply_convert_fusion.4
  497.4 4.4 fusion.10
  501.8 1.3 collective-permute-start
  504.5 13.1 %collective-permute-done = bf16[32,8192]{1,0:T(8,128)(2,1)S(1)} collective-permute-done((bf16[32,8192]{1,0:T(8,128)(2,1)S(1)}, bf16[32,8192]{1,0:T(8,128)(2,1)S(1)}, u32[]{:S(2)}, u32[]{:S(2)}) %collective-permute-start) | collective-permute-done | bytes 524320 | tf_op jit(solution)/shard_map/while/body/eval_jaxpr/ppermute | solution.py:12
  517.7 1.3 collective-permute-start
  520.4 12.3 %collective-permute-done = bf16[32,8192]{1,0:T(8,128)(2,1)S(1)} collective-permute-done((bf16[32,8192]{1,0:T(8,128)(2,1)S(1)}, bf16[32,8192]{1,0:T(8,128)(2,1)S(1)}, u32[]{:S(2)}, u32[]{:S(2)}) %collective-permute-start) | collective-permute-done | bytes 524320 | tf_op jit(solution)/shard_map/while/body/eval_jaxpr/ppermute | solution.py:12
  532.8 1.3 collective-permute-start
  535.5 11.4 %collective-permute-done = bf16[32,8192]{1,0:T(8,128)(2,1)S(1)} collective-permute-done((bf16[32,8192]{1,0:T(8,128)(2,1)S(1)}, bf16[32,8192]{1,0:T(8,128)(2,1)S(1)}, u32[]{:S(2)}, u32[]{:S(2)}) %collective-permute-start) | collective-permute-done | bytes 524320 | tf_op jit(solution)/shard_map/while/body/eval_jaxpr/ppermute | solution.py:12
  547.0 1.3 collective-permute-start
  549.7 27.3 %collective-permute-done = bf16[32,8192]{1,0:T(8,128)(2,1)S(1)} collective-permute-done((bf16[32,8192]{1,0:T(8,128)(2,1)S(1)}, bf16[32,8192]{1,0:T(8,128)(2,1)S(1)}, u32[]{:S(2)}, u32[]{:S(2)}) %collective-permute-start) | collective-permute-done | bytes 524320 | tf_op jit(solution)/shard_map/while/body/eval_jaxpr/ppermute | solution.py:12
  577.0 20.4 %conditional.4 = (f32[4,1024,128]{2,1,0:T(8,128)}) conditional(s32[]{:T(128)} %convert_element_type.143, f32[4,1024,128]{2,1,0:T(8,128)} %get-tuple-element.272, (bf16[32,8192]{1,0:T(8,128)(2,1)S(1)}, bf16[32,8192]{1,0:T(8,128)(2,1)S(1)}, bf16[8192,128]{1,0:T(8,128)(2,1)}, pred[4]{0:T(512)(128)(4,1)S(1)}, f32[4,1024,128]{2,1,0:T(8,128)}) %tuple.71), branch_computations={%region_7.7_spmd, %region_8.0_spmd} | conditional | flops 2165309440 | bytes 44564540 | solution.py:67
  578.3 2.3 fusion.14
  581.7 2.3 convolution_add_fusion.5
  585.1 2.3 convolution_add_fusion.4
  587.4 3.0 multiply_convert_fusion.4
  593.1 4.4 fusion.10
  597.5 1.3 collective-permute-start
  600.2 8.4 %collective-permute-done = bf16[32,8192]{1,0:T(8,128)(2,1)S(1)} collective-permute-done((bf16[32,8192]{1,0:T(8,128)(2,1)S(1)}, bf16[32,8192]{1,0:T(8,128)(2,1)S(1)}, u32[]{:S(2)}, u32[]{:S(2)}) %collective-permute-start) | collective-permute-done | bytes 524320 | tf_op jit(solution)/shard_map/while/body/eval_jaxpr/ppermute | solution.py:12
  (72 shorter events, 28.0 us)
Async XLA Ops:
  6.5 1.4 copy-start
  6.5 103.4 %copy-start.7 = (s32[1,1,4]{2,1,0:T(1,128)S(1)}, s32[1,1,4]{2,1,0:T(1,128)}, u32[]{:S(2)}) copy-start(s32[1,1,4]{2,1,0:T(1,128)} %param.17) | copy-start | bytes 52
  6.5 104.8 %copy-start.1 = (bf16[32,8192]{1,0:T(8,128)(2,1)S(1)}, bf16[32,8192]{1,0:T(8,128)(2,1)}, u32[]{:S(2)}) copy-start(bf16[32,8192]{1,0:T(8,128)(2,1)} %param.16) | copy-start | bytes 1572868
  6.5 187.9 %all-gather.2.cloned.1.call-start = ((), (), s32[]{:S(2)}) async-start(), calls=%async_computation | async-start | bytes 2228224 | tf_op jit(solution)/shard_map/all_gather | solution.py:52
  195.9 4.1 copy-start.6
  200.0 39.5 %collective-permute-start = (bf16[32,8192]{1,0:T(8,128)(2,1)S(1)}, bf16[32,8192]{1,0:T(8,128)(2,1)S(1)}, u32[]{:S(2)}, u32[]{:S(2)}) collective-permute-start(bf16[32,8192]{1,0:T(8,128)(2,1)S(1)} %get-tuple-element.271), channel_id=1, source_target_pairs={{4,0},{8,4},{12,8},{16,12},{20,16},{24,20},{28,24},{32,28},{36,32}... | collective-permute-start | bytes 1572872 | tf_op jit(solution)/shard_map/while/body/eval_jaxpr/ppermute | solution.py:12
  239.6 39.7 %collective-permute-start = (bf16[32,8192]{1,0:T(8,128)(2,1)S(1)}, bf16[32,8192]{1,0:T(8,128)(2,1)S(1)}, u32[]{:S(2)}, u32[]{:S(2)}) collective-permute-start(bf16[32,8192]{1,0:T(8,128)(2,1)S(1)} %get-tuple-element.271), channel_id=1, source_target_pairs={{4,0},{8,4},{12,8},{16,12},{20,16},{24,20},{28,24},{32,28},{36,32}... | collective-permute-start | bytes 1572872 | tf_op jit(solution)/shard_map/while/body/eval_jaxpr/ppermute | solution.py:12
  279.4 15.3 %collective-permute-start = (bf16[32,8192]{1,0:T(8,128)(2,1)S(1)}, bf16[32,8192]{1,0:T(8,128)(2,1)S(1)}, u32[]{:S(2)}, u32[]{:S(2)}) collective-permute-start(bf16[32,8192]{1,0:T(8,128)(2,1)S(1)} %get-tuple-element.271), channel_id=1, source_target_pairs={{4,0},{8,4},{12,8},{16,12},{20,16},{24,20},{28,24},{32,28},{36,32}... | collective-permute-start | bytes 1572872 | tf_op jit(solution)/shard_map/while/body/eval_jaxpr/ppermute | solution.py:12
  294.8 11.1 %collective-permute-start = (bf16[32,8192]{1,0:T(8,128)(2,1)S(1)}, bf16[32,8192]{1,0:T(8,128)(2,1)S(1)}, u32[]{:S(2)}, u32[]{:S(2)}) collective-permute-start(bf16[32,8192]{1,0:T(8,128)(2,1)S(1)} %get-tuple-element.271), channel_id=1, source_target_pairs={{4,0},{8,4},{12,8},{16,12},{20,16},{24,20},{28,24},{32,28},{36,32}... | collective-permute-start | bytes 1572872 | tf_op jit(solution)/shard_map/while/body/eval_jaxpr/ppermute | solution.py:12
  305.9 24.5 %collective-permute-start = (bf16[32,8192]{1,0:T(8,128)(2,1)S(1)}, bf16[32,8192]{1,0:T(8,128)(2,1)S(1)}, u32[]{:S(2)}, u32[]{:S(2)}) collective-permute-start(bf16[32,8192]{1,0:T(8,128)(2,1)S(1)} %get-tuple-element.271), channel_id=1, source_target_pairs={{4,0},{8,4},{12,8},{16,12},{20,16},{24,20},{28,24},{32,28},{36,32}... | collective-permute-start | bytes 1572872 | tf_op jit(solution)/shard_map/while/body/eval_jaxpr/ppermute | solution.py:12
  330.5 15.5 %collective-permute-start = (bf16[32,8192]{1,0:T(8,128)(2,1)S(1)}, bf16[32,8192]{1,0:T(8,128)(2,1)S(1)}, u32[]{:S(2)}, u32[]{:S(2)}) collective-permute-start(bf16[32,8192]{1,0:T(8,128)(2,1)S(1)} %get-tuple-element.271), channel_id=1, source_target_pairs={{4,0},{8,4},{12,8},{16,12},{20,16},{24,20},{28,24},{32,28},{36,32}... | collective-permute-start | bytes 1572872 | tf_op jit(solution)/shard_map/while/body/eval_jaxpr/ppermute | solution.py:12
  346.0 25.6 %collective-permute-start = (bf16[32,8192]{1,0:T(8,128)(2,1)S(1)}, bf16[32,8192]{1,0:T(8,128)(2,1)S(1)}, u32[]{:S(2)}, u32[]{:S(2)}) collective-permute-start(bf16[32,8192]{1,0:T(8,128)(2,1)S(1)} %get-tuple-element.271), channel_id=1, source_target_pairs={{4,0},{8,4},{12,8},{16,12},{20,16},{24,20},{28,24},{32,28},{36,32}... | collective-permute-start | bytes 1572872 | tf_op jit(solution)/shard_map/while/body/eval_jaxpr/ppermute | solution.py:12
  392.2 13.9 %collective-permute-start = (bf16[32,8192]{1,0:T(8,128)(2,1)S(1)}, bf16[32,8192]{1,0:T(8,128)(2,1)S(1)}, u32[]{:S(2)}, u32[]{:S(2)}) collective-permute-start(bf16[32,8192]{1,0:T(8,128)(2,1)S(1)} %get-tuple-element.271), channel_id=1, source_target_pairs={{4,0},{8,4},{12,8},{16,12},{20,16},{24,20},{28,24},{32,28},{36,32}... | collective-permute-start | bytes 1572872 | tf_op jit(solution)/shard_map/while/body/eval_jaxpr/ppermute | solution.py:12
  406.1 38.8 %collective-permute-start = (bf16[32,8192]{1,0:T(8,128)(2,1)S(1)}, bf16[32,8192]{1,0:T(8,128)(2,1)S(1)}, u32[]{:S(2)}, u32[]{:S(2)}) collective-permute-start(bf16[32,8192]{1,0:T(8,128)(2,1)S(1)} %get-tuple-element.271), channel_id=1, source_target_pairs={{4,0},{8,4},{12,8},{16,12},{20,16},{24,20},{28,24},{32,28},{36,32}... | collective-permute-start | bytes 1572872 | tf_op jit(solution)/shard_map/while/body/eval_jaxpr/ppermute | solution.py:12
  465.4 15.9 %collective-permute-start = (bf16[32,8192]{1,0:T(8,128)(2,1)S(1)}, bf16[32,8192]{1,0:T(8,128)(2,1)S(1)}, u32[]{:S(2)}, u32[]{:S(2)}) collective-permute-start(bf16[32,8192]{1,0:T(8,128)(2,1)S(1)} %get-tuple-element.271), channel_id=1, source_target_pairs={{4,0},{8,4},{12,8},{16,12},{20,16},{24,20},{28,24},{32,28},{36,32}... | collective-permute-start | bytes 1572872 | tf_op jit(solution)/shard_map/while/body/eval_jaxpr/ppermute | solution.py:12
  501.8 15.9 %collective-permute-start = (bf16[32,8192]{1,0:T(8,128)(2,1)S(1)}, bf16[32,8192]{1,0:T(8,128)(2,1)S(1)}, u32[]{:S(2)}, u32[]{:S(2)}) collective-permute-start(bf16[32,8192]{1,0:T(8,128)(2,1)S(1)} %get-tuple-element.271), channel_id=1, source_target_pairs={{4,0},{8,4},{12,8},{16,12},{20,16},{24,20},{28,24},{32,28},{36,32}... | collective-permute-start | bytes 1572872 | tf_op jit(solution)/shard_map/while/body/eval_jaxpr/ppermute | solution.py:12
  517.7 15.0 %collective-permute-start = (bf16[32,8192]{1,0:T(8,128)(2,1)S(1)}, bf16[32,8192]{1,0:T(8,128)(2,1)S(1)}, u32[]{:S(2)}, u32[]{:S(2)}) collective-permute-start(bf16[32,8192]{1,0:T(8,128)(2,1)S(1)} %get-tuple-element.271), channel_id=1, source_target_pairs={{4,0},{8,4},{12,8},{16,12},{20,16},{24,20},{28,24},{32,28},{36,32}... | collective-permute-start | bytes 1572872 | tf_op jit(solution)/shard_map/while/body/eval_jaxpr/ppermute | solution.py:12
  532.8 14.1 %collective-permute-start = (bf16[32,8192]{1,0:T(8,128)(2,1)S(1)}, bf16[32,8192]{1,0:T(8,128)(2,1)S(1)}, u32[]{:S(2)}, u32[]{:S(2)}) collective-permute-start(bf16[32,8192]{1,0:T(8,128)(2,1)S(1)} %get-tuple-element.271), channel_id=1, source_target_pairs={{4,0},{8,4},{12,8},{16,12},{20,16},{24,20},{28,24},{32,28},{36,32}... | collective-permute-start | bytes 1572872 | tf_op jit(solution)/shard_map/while/body/eval_jaxpr/ppermute | solution.py:12
  547.0 30.0 %collective-permute-start = (bf16[32,8192]{1,0:T(8,128)(2,1)S(1)}, bf16[32,8192]{1,0:T(8,128)(2,1)S(1)}, u32[]{:S(2)}, u32[]{:S(2)}) collective-permute-start(bf16[32,8192]{1,0:T(8,128)(2,1)S(1)} %get-tuple-element.271), channel_id=1, source_target_pairs={{4,0},{8,4},{12,8},{16,12},{20,16},{24,20},{28,24},{32,28},{36,32}... | collective-permute-start | bytes 1572872 | tf_op jit(solution)/shard_map/while/body/eval_jaxpr/ppermute | solution.py:12
  597.5 11.1 %collective-permute-start = (bf16[32,8192]{1,0:T(8,128)(2,1)S(1)}, bf16[32,8192]{1,0:T(8,128)(2,1)S(1)}, u32[]{:S(2)}, u32[]{:S(2)}) collective-permute-start(bf16[32,8192]{1,0:T(8,128)(2,1)S(1)} %get-tuple-element.271), channel_id=1, source_target_pairs={{4,0},{8,4},{12,8},{16,12},{20,16},{24,20},{28,24},{32,28},{36,32}... | collective-permute-start | bytes 1572872 | tf_op jit(solution)/shard_map/while/body/eval_jaxpr/ppermute | solution.py:12
Sparse Core Ops, SparseCore 0:
  110.0 84.3 all-gather.1
where the time goes:
time: 617 us; the launch traced here: 615 us
  waiting for transfers between devices  368 us (60%)
  blocking collectives  99.6 us (16%)
  matrix products  48.2 us (8%)
  other arithmetic  40.1 us (6%)
  starting transfers between devices  19.4 us (3%)
  loops' own time  18.7 us (3%)
  between operations  14.1 us (2%)
  local copies, waits for them, and re-layouts  7.63 us (1%)
    ppermute x15, waiting for transfers between devices, shifted(): return lax.ppermute(block, axis, route)  285 us
    psum x1, blocking collectives, on_device(): summed = lax.psum(partial_mix, ('grp', 'val'))  99.6 us
    all_gather x1, waiting for transfers between devices, on_device(): lax.all_gather(own_mixed.astype(jnp.bfloat16), 'cond', axis=0, tiled=True)  82.3 us
    dot_general x16, matrix products, pair_kernel(): jnp.dot(density, mixed[offset:offset + point_block], preferred_element_ty...  45.2 us
    convert_element_type x16, other arithmetic, pair_kernel(): density = (left_part[:, None, :] * right_part[None, :, :]).reshape(band_b...  24.9 us
    ppermute x15, starting transfers between devices, shifted(): return lax.ppermute(block, axis, route)  19.4 us
  transfers between devices with their start and end apart: 16, of which 16 were waited for; matrix products, arithmetic and copies ran while one was open for 2% of the time, Pallas kernels for 0%

commit v1 on v0

v1 whole, which is shorter than its diff:
```python
import math

import jax
import jax.numpy as jnp
from jax import lax
from jax.experimental import pallas as pl
from jax.experimental.pallas import tpu as pltpu
from jax.sharding import PartitionSpec as P

CHUNK = 1024


def blocks_kernel(partners_ref, left_ref, right_ref, mixed_ref, out_ref):
    bands = left_ref.shape[0]
    points = left_ref.shape[1]
    slots = right_ref.shape[0] // bands
    out_ref[...] = jnp.zeros_like(out_ref)

    def step(i, carry):
        part = pl.ds(pl.multiple_of(i * CHUNK, CHUNK), CHUNK)
        mixed = mixed_ref[part, :]
        for s in range(slots):
            right = right_ref[s * bands : (s + 1) * bands, part]
            rows = [
                jnp.broadcast_to(left_ref[x : x + 1, part], right.shape) * right
                for x in range(bands)
            ]
            density = jnp.concatenate(rows, 0)
            out_ref[s] += jnp.dot(density, mixed, preferred_element_type=jnp.float32)
        return carry

    lax.fori_loop(0, points // CHUNK, step, 0)
    for s in range(slots):
        scale = jnp.where(partners_ref[s] >= 0, 1.0 / math.sqrt(points), 0.0)
        out_ref[s] = out_ref[s] * scale


def on_device(screened, valence, first_band, second_band, conduction, partners):
    band_count = valence.shape[1]
    bands = conduction.shape[0]
    points = conduction.shape[1]
    band_index = lax.broadcasted_iota(jnp.int32, (band_count, first_band.shape[0]), 0)
    first_cols = jnp.dot(
        valence,
        (band_index == first_band[None, :]).astype(jnp.bfloat16),
        preferred_element_type=jnp.float32,
    )
    second_cols = jnp.dot(
        valence,
        (band_index == second_band[None, :]).astype(jnp.bfloat16),
        preferred_element_type=jnp.float32,
    )
    pair_density = (first_cols * second_cols).astype(jnp.bfloat16)
    partial_mix = jnp.dot(screened, pair_density, preferred_element_type=jnp.float32)
    own = lax.psum_scatter(partial_mix, "val", scatter_dimension=1, tiled=True)
    own = lax.psum(own, "grp")
    mixed = lax.all_gather(own.astype(jnp.bfloat16), "cond", axis=0, tiled=True)
    every = lax.all_gather(conduction, "cond", axis=0, tiled=True)
    owned = partners.reshape(-1)
    right = jnp.concatenate(
        [
            lax.dynamic_slice_in_dim(every, jnp.maximum(owned[s], 0) * bands, bands, 0)
            for s in range(owned.shape[0])
        ],
        0,
    )
    vmem = pl.BlockSpec(memory_space=pltpu.VMEM)
    kernel = pl.pallas_call(
        blocks_kernel,
        out_shape=jax.ShapeDtypeStruct(
            (owned.shape[0], bands * bands, mixed.shape[1]), jnp.float32
        ),
        in_specs=[pl.BlockSpec(memory_space=pltpu.SMEM), vmem, vmem, vmem],
        out_specs=vmem,
        compiler_params=pltpu.CompilerParams(vmem_limit_bytes=48 * 2**20),
    )(owned, conduction, right, mixed)
    return kernel.reshape((1, 1) + kernel.shape)


def solution(mesh):
    in_specs = (
        P("cond", ("grp", "val")),
        P(("grp", "val"), None),
        P(),
        P(),
        P("cond", None),
        P("grp", "cond", None),
    )
    out_specs = P("grp", "cond", None, None, "val")
    return jax.shard_map(
        on_device, mesh=mesh, in_specs=in_specs, out_specs=out_specs, check_vma=False
    )
```

time: 617 us -> 250 us (0.41)
  waiting for transfers between devices: 368 us -> 172 us
  blocking collectives: 99.6 us -> 31.5 us
  matrix products: 48.2 us -> 4.05 us
  other arithmetic: 40.1 us -> 0.14 us
  Pallas kernels: 0 us -> 21.1 us
  starting transfers between devices: 19.4 us -> 0.09 us
  loops' own time: 18.7 us -> 0 us
    ppermute x15 -> x0, waiting for transfers between devices: 285 us -> none  [shifted(): return lax.ppermute(block, axis, route)]
    psum x1, blocking collectives: 99.6 us -> 31.5 us  [on_device(): own = lax.psum(own, 'grp')]
    all_gather x1 -> x2, waiting for transfers between devices: 82.3 us -> 145 us  [the longest x1 93.7 us: on_device(): mixed = lax.all_gather(own.astype(jnp.bfloat16), 'cond', axis=0, tiled=True)]
    dot_general x16 -> x0, matrix products: 45.2 us -> none  [pair_kernel(): jnp.dot(density, mixed[offset:offset + point_block], preferred_element_ty...]
    reduce_scatter x0 -> x1, waiting for transfers between devices: none -> 26.5 us  [on_device(): own = lax.psum_scatter(partial_mix, 'val', scatter_dimension=1, tiled=True)]
    convert_element_type x20 -> x0, other arithmetic: 25.9 us -> none  [the longest x16 24.9 us: pair_kernel(): density = (left_part[:, None, :] * right_part[None, :, :]).reshape(band_b...]
    pallas_call x0 -> x1, Pallas kernels: none -> 21.1 us  [on_device(): pl.pallas_call(blocks_kernel, out_shape=jax.ShapeDtypeStruct((owned.shape...]
    ppermute x15 -> x0, starting transfers between devices: 19.4 us -> none  [shifted(): return lax.ppermute(block, axis, route)]
  transfers between devices with their start and end apart: 16 -> 3, of which waited for: 16 -> 3; matrix products, arithmetic and copies ran while one was open for 2% -> 1% of each run, Pallas kernels for 0% -> 0%
where the time goes in v1:
time: 250 us
  waiting for transfers between devices  172 us (69%)
  blocking collectives  31.5 us (13%)
  Pallas kernels  21.1 us (8%)
  between operations  17.3 us (7%)
  matrix products  4.05 us (2%)
  local copies, waits for them, and re-layouts  3.92 us (2%)
    all_gather x1, waiting for transfers between devices, on_device(): mixed = lax.all_gather(own.astype(jnp.bfloat16), 'cond', axis=0, tiled=True)  93.7 us
    all_gather x1, waiting for transfers between devices, on_device(): every = lax.all_gather(conduction, 'cond', axis=0, tiled=True)  50.8 us
    psum x1, blocking collectives, on_device(): own = lax.psum(own, 'grp')  31.5 us
    reduce_scatter x1, waiting for transfers between devices, on_device(): own = lax.psum_scatter(partial_mix, 'val', scatter_dimension=1, tiled=True)  26.5 us
    pallas_call x1, Pallas kernels, on_device(): pl.pallas_call(blocks_kernel, out_shape=jax.ShapeDtypeStruct((owned.shape...  21.1 us
  transfers between devices with their start and end apart: 3, of which 3 were waited for; matrix products, arithmetic and copies ran while one was open for 1% of the time, Pallas kernels for 0%

profile of v1, /device:TPU:8, one launch (start us, length us, event | category | flops | bytes accessed | tf_op | source)
XLA Modules:
  0.0 249.7 jit_solution(12897102693562069482)
XLA Ops:
  7.4 0.0 copy-start
  7.4 0.0 copy-start.3
  7.4 0.0 reduce-scatter.2.cloned.1.call-start
  7.4 1.4 fusion.5
  8.8 0.0 copy-done
  8.8 2.7 %convolution_bitcast_fusion = f32[512,512]{1,0:T(8,128)} fusion(bf16[512,512]{1,0:T(8,128)(2,1)S(1)} %copy-done, f32[512,512]{1,0:T(8,128)S(1)} %fusion.5, bf16[512,256]{1,0:T(8,128)(2,1)} %param.7, s32[512]{0:T(512)} %param.9), kind=kOutput, calls=%fused_computation.1 | convolution fusion | flops 403439616 | bytes 2885632 | tf_op jit(solution)/shard_map/dot_general | solution.py:54
  11.4 0.0 reduce-scatter.2.cloned.1.call-update
  11.5 0.0 all-gather.3.cloned.1.call-start
  11.5 0.5 all-gather.3.cloned.1.call-update
  12.0 0.0 all-gather.5.cloned.1.call-start
  12.1 26.5 %reduce-scatter.2.cloned.1.call-done = f32[512,128]{1,0:T(8,128)} async-done(((f32[512,512]{1,0:T(8,128)}), f32[512,128]{1,0:T(8,128)}) %reduce-scatter.2.cloned.1.call-update) | async-done | bytes 262160 | tf_op jit(solution)/shard_map/reduce_scatter | solution.py:55
  38.6 31.5 %all-reduce.1 = bf16[512,128]{1,0:T(8,128)(2,1)} all-reduce(f32[512,128]{1,0:T(8,128)} %reduce-scatter.2.cloned.1.call-done), channel_id=1, replica_groups=mesh['grp'=4,'cond'=16,'val'=4] {'grp'}, use_global_device_ids=true, to_apply=%region_1.0 | all-reduce | flops 65536 | bytes 393216 | tf_op jit(solution)/shard_map/psum | solution.py:56
  70.1 0.0 all-gather.5.cloned.1.call-update
  70.1 0.0 copy-done.3
  70.1 0.6 fusion.10
  73.2 0.0 copy-start.2
  73.2 50.8 %all-gather.3.cloned.1.call-done = bf16[512,8192]{1,0:T(8,128)(2,1)} async-done(((bf16[32,8192]{1,0:T(8,128)(2,1)}), bf16[512,8192]{1,0:T(8,128)(2,1)}) %all-gather.3.cloned.1.call-update) | async-done | bytes 8388624 | tf_op jit(solution)/shard_map/all_gather | solution.py:58
  124.0 1.7 constant_dynamic-slice_fusion.3
  125.7 0.1 pad_maximum_fusion.right_ref
  125.8 93.7 %all-gather.5.cloned.1.call-done.mixed_ref = bf16[8192,128]{1,0:T(8,128)(2,1)} async-done(((bf16[512,128]{1,0:T(8,128)(2,1)}), bf16[8192,128]{1,0:T(8,128)(2,1)}) %all-gather.5.cloned.1.call-update) | async-done | bytes 2097168 | tf_op jit(solution)/shard_map/all_gather | solution.py:57
  219.6 0.0 copy-done.2
  219.6 0.0 copy-start.1
  219.6 1.6 copy-done.1
  221.2 21.1 %shard_map.64 = f32[4,1024,128]{2,1,0:T(8,128)} custom-call(s32[4]{0:T(128)S(1)} %bitcast.11, bf16[32,8192]{1,0:T(8,128)(2,1)S(1)} %copy-done.2, bf16[128,8192]{1,0:T(8,128)(2,1)S(1)} %pad_maximum_fusion.right_ref, bf16[8192,128]{1,0:T(8,128)(2,1)S(1)} %copy-done.1), custom_call_target="tpu_custom_call" | custom-call | tf_op jit(solution)/shard_map/pallas_call | solution.py:68
Async XLA Ops:
  7.4 1.4 copy-start
  7.4 62.8 %copy-start.3 = (s32[1,1,4]{2,1,0:T(1,128)S(1)}, s32[1,1,4]{2,1,0:T(1,128)}, u32[]{:S(2)}) copy-start(s32[1,1,4]{2,1,0:T(1,128)} %param.11) | copy-start | bytes 52
  7.4 31.2 %reduce-scatter.2.cloned.1.call-start = ((), (), s32[]{:S(2)}) async-start(), calls=%async_computation.2 | async-start | bytes 1310720 | tf_op jit(solution)/shard_map/reduce_scatter | solution.py:55
  11.5 112.5 %all-gather.3.cloned.1.call-start = ((), (), s32[]{:S(2)}) async-start(), calls=%async_computation.1 | async-start | bytes 8912896 | tf_op jit(solution)/shard_map/all_gather | solution.py:58
  12.0 207.5 %all-gather.5.cloned.1.call-start = ((), (), s32[]{:S(2)}) async-start(), calls=%async_computation.3 | async-start | bytes 2228224 | tf_op jit(solution)/shard_map/all_gather | solution.py:57
  73.2 146.4 %copy-start.2 = (bf16[32,8192]{1,0:T(8,128)(2,1)S(1)}, bf16[32,8192]{1,0:T(8,128)(2,1)}, u32[]{:S(2)}) copy-start(bf16[32,8192]{1,0:T(8,128)(2,1)} %left_ref.1) | copy-start | bytes 1572868
  219.6 1.6 copy-start.1
Sparse Core Ops, SparseCore 0:
  11.6 26.9 reduce-scatter.1
Sparse Core Ops, SparseCore 1:
  13.7 110.2 all-gather.2
  125.8 93.7 all-gather.4

commit v2 on v1

v2 whole, which is shorter than its diff:
```python
import math

import jax
import jax.numpy as jnp
from jax import lax
from jax.experimental import pallas as pl
from jax.experimental.pallas import tpu as pltpu
from jax.sharding import PartitionSpec as P

MESH = pl.DeviceIdType.MESH
BF16 = jnp.bfloat16
F32 = jnp.float32
SIDE = 4
BANDS = 32
SLOTS = 4
POINTS = 8192
PAIRS = 512
OWN_PAIRS = 128
HALF_ROWS = 256
PIECE = 1024


def whole_kernel(
    partners_ref,
    first_ref,
    second_ref,
    screened_ref,
    valence_ref,
    conduction_ref,
    out_ref,
    left,
    scr,
    val,
    dens,
    sums,
    tosend,
    parts,
    zout,
    zin,
    gath,
    mix,
    sel,
    loc_sem,
    pair_send,
    pair_recv,
    y_send,
    y_recv,
    z_send,
    z_recv,
    ga_send,
    ga_recv,
    gb_send,
    gb_recv,
    gs_send,
    gs_recv,
    ma_send,
    ma_recv,
    mb_send,
    mb_recv,
    ms_send,
    ms_recv,
    sel_send,
    sel_recv,
):
    grp = lax.axis_index("grp")
    cond = lax.axis_index("cond")
    y = lax.axis_index("val")
    core = lax.rem(grp, 2)
    x = lax.rem(cond, SIDE)
    zlo = cond // SIDE
    z = (grp // 2) * SIDE + zlo
    par = lax.rem(x, 2)

    def device(px, py, pz, pcore):
        px = lax.rem(px + SIDE, SIDE)
        py = lax.rem(py + SIDE, SIDE)
        pz = lax.rem(pz + 2 * SIDE, 2 * SIDE)
        return ((pz // SIDE) * 2 + pcore, lax.rem(pz, SIDE) * SIDE + px, py)

    sibling = device(x, y, z, 1 - core)
    opposite = device(x, y, z + SIDE, core)

    def y_peer(j):
        return device(x, y + j, z, core)

    def z_step(j, up):
        return (0, 1, up * 4 - 2, -1)[j]

    pa = x * (1 - core) + zlo * core
    pb = zlo * (1 - core) + x * core

    def peer_a(j):
        return device(x + j * (1 - core), y, z + z_step(j, par) * core, core)

    def peer_b(j, up):
        return device(x + j * core, y, z + z_step(j, up) * (1 - core), core)

    def back(p, j):
        return lax.rem(p + SIDE - j, SIDE)

    def remote(src, dst, ssem, rsem, dev):
        return pltpu.make_async_remote_copy(
            src_ref=src, dst_ref=dst, send_sem=ssem, recv_sem=rsem, device_id=dev,
            device_id_type=MESH,
        )

    own_rows = pl.ds(pl.multiple_of(core * HALF_ROWS, HALF_ROWS), HALF_ROWS)
    other_rows = pl.ds(pl.multiple_of((1 - core) * HALF_ROWS, HALF_ROWS), HALF_ROWS)
    own_points = pl.ds(pl.multiple_of(y * 2 * PIECE + core * PIECE, PIECE), PIECE)
    load_val = pltpu.make_async_copy(valence_ref, val.at[core], loc_sem.at[0])
    load_scr = pltpu.make_async_copy(screened_ref.at[own_rows, :], scr.at[core], loc_sem.at[1])
    load_gath = pltpu.make_async_copy(
        conduction_ref.at[:, own_points], gath.at[core, pb, pa], loc_sem.at[2]
    )
    load_left = pltpu.make_async_copy(conduction_ref, left, loc_sem.at[3])
    for load in (load_val, load_scr, load_gath, load_left):
        load.start()

    peers = [sibling, opposite]
    peers += [y_peer(j) for j in (1, 2, 3)]
    peers += [device(x + j, y, z, core) for j in (1, 2, 3)]
    peers += [device(x, y, z + j, core) for j in (1, -1, 2, -2)]
    barrier = pltpu.get_barrier_semaphore()
    for peer in peers:
        pl.semaphore_signal(barrier, inc=1, device_id=peer, device_id_type=MESH)
    pl.semaphore_wait(barrier, len(peers))

    give_val = remote(valence_ref, val.at[core], pair_send.at[0], pair_recv.at[0], sibling)
    give_scr = remote(
        screened_ref.at[other_rows, :], scr.at[core], pair_send.at[1], pair_recv.at[1], sibling
    )
    give_val.start()
    give_scr.start()

    def gather(buf, own, send_a, recv_a, send_b, recv_b, send_s, recv_s):
        low, high = pl.ds(0, 2), pl.ds(2, 2)

        def step_a(j):
            return remote(
                own, buf.at[core, pb, pa], send_a.at[j - 1], recv_a.at[j - 1], peer_a(j)
            )

        def got_a(j):
            place = buf.at[core, pb, back(pa, j)]
            return remote(place, place, send_a.at[j - 1], recv_a.at[j - 1], peer_a(j))

        def step_b(i):
            if i < 2:
                place = buf.at[core, pb]
                return remote(place, place, send_b.at[i], recv_b.at[i], peer_b((1, 3)[i], 0))
            place = buf.at[core, pb, (low, high)[i - 2]]
            return remote(place, place, send_b.at[i], recv_b.at[i], peer_b(2, i - 2))

        def got_b(i):
            if i < 2:
                place = buf.at[core, back(pb, (1, 3)[i])]
            else:
                place = buf.at[core, back(pb, 2), (low, high)[i - 2]]
            return remote(place, place, send_b.at[i], recv_b.at[i], sibling)

        def step_s(i):
            place = buf.at[core, back(pb, (0, 1, 3, 2)[i])]
            return remote(place, place, send_s.at[i], recv_s.at[i], sibling)

        def got_s(i):
            place = buf.at[1 - core, i]
            return remote(place, place, send_s.at[i], recv_s.at[i], sibling)

        def start_a():
            for j in (1, 3, 2):
                step_a(j).start()

        def a_to_b():
            for j in (1, 3, 2):
                got_a(j).wait_recv()
            for i in range(4):
                step_b(i).start()
            step_s(0).start()

        def b_to_s():
            for i in range(2):
                got_b(i).wait_recv()
                step_s(i + 1).start()
            for i in range(2, 4):
                got_b(i).wait_recv()
            step_s(3).start()

        def finish_s():
            for i in range(4):
                got_s(i).wait_recv()

        def drain():
            for j in (1, 2, 3):
                step_a(j).wait_send()
            for i in range(4):
                step_b(i).wait_send()
                step_s(i).wait_send()

        return start_a, a_to_b, b_to_s, finish_s, drain

    cond_a, cond_ab, cond_bs, cond_s, cond_drain = gather(
        gath, conduction_ref.at[:, own_points], ga_send, ga_recv, gb_send, gb_recv, gs_send, gs_recv
    )
    cond_a()

    band = lax.broadcasted_iota(jnp.int32, (val.shape[2], PAIRS), 0)
    first_pick = jnp.where(band == first_ref[...], 1.0, 0.0).astype(BF16)
    second_pick = jnp.where(band == second_ref[...], 1.0, 0.0).astype(BF16)

    def densities(which):
        for part in range(2):
            rows = pl.ds(part * 256, 256)
            points = val[which, rows, :]
            first_cols = jnp.dot(points, first_pick, preferred_element_type=F32)
            second_cols = jnp.dot(points, second_pick, preferred_element_type=F32)
            dens[which, rows, :] = (first_cols * second_cols).astype(BF16)

    load_val.wait()
    densities(core)
    give_val.wait_recv()
    densities(1 - core)

    load_gath.wait()
    cond_ab()

    load_scr.wait()
    give_scr.wait_recv()
    for v in range(SIDE):
        cols = pl.ds(v * OWN_PAIRS, OWN_PAIRS)
        total = jnp.dot(scr[0], dens[0, :, cols], preferred_element_type=F32)
        total += jnp.dot(scr[1], dens[1, :, cols], preferred_element_type=F32)
        sums[v] = total
        tosend[v] = total.astype(BF16)

    def y_step(j):
        return remote(
            tosend.at[lax.rem(y + j, SIDE)], parts.at[j - 1], y_send.at[j - 1], y_recv.at[j - 1],
            y_peer(j),
        )

    for j in (1, 3, 2):
        y_step(j).start()
    for j in (1, 3, 2):
        y_step(j).wait_recv()
    summed = sums[y]
    for j in (1, 2, 3):
        summed += parts[j - 1].astype(F32)
    zout[...] = summed.astype(BF16)
    sums[0] = summed
    z_copy = remote(zout, zin, z_send, z_recv, opposite)
    z_copy.start()

    cond_bs()
    cond_s()
    for s in range(SLOTS):
        block = jnp.maximum(partners_ref[s], 0)
        block_z = block // SIDE
        block_x = lax.rem(block, SIDE)
        rows = pl.ds(s * BANDS, BANDS)
        sel[y, 0, rows, :] = gath[0, block_z, block_x]
        sel[y, 1, rows, :] = gath[1, block_x, block_z]

    def sel_step(j, h):
        place = sel.at[y, h]
        return remote(place, place, sel_send.at[j - 1, h], sel_recv.at[j - 1, h], y_peer(j))

    for h in range(2):
        for j in (1, 3):
            sel_step(j, h).start()
    for h in range(2):
        sel_step(2, h).start()

    z_copy.wait_recv()
    mix[core, pb, pa] = (sums[0] + zin[...].astype(F32)).astype(BF16)
    mix_a, mix_ab, mix_bs, mix_s, mix_drain = gather(
        mix, mix.at[core, pb, pa], ma_send, ma_recv, mb_send, mb_recv, ms_send, ms_recv
    )
    mix_a()
    out_ref[...] = jnp.zeros_like(out_ref)
    load_left.wait()
    mix_ab()
    mix_bs()
    mix_s()

    def unit(u, carry):
        step = u // 2
        half = lax.rem(u, 2)
        ahead = step + step // 2 - 2 * (step // 3)
        q = lax.rem(y + ahead, SIDE)

        @pl.when(step > 0)
        def _():
            sender = lax.rem(SIDE - ahead, SIDE)
            place = sel.at[q, half]
            remote(
                place, place, sel_send.at[sender - 1, half], sel_recv.at[sender - 1, half], sibling
            ).wait_recv()

        mixed = jnp.concatenate(
            [
                mix[0, q, 2 * half],
                mix[1, 2 * half, q],
                mix[0, q, 2 * half + 1],
                mix[1, 2 * half + 1, q],
            ],
            0,
        )
        points = pl.ds(pl.multiple_of(q * 2 * PIECE + half * PIECE, PIECE), PIECE)
        for s in range(SLOTS):
            right = sel[q, half, s * BANDS : (s + 1) * BANDS, :]
            rows = [
                jnp.broadcast_to(left[i : i + 1, points], right.shape) * right
                for i in range(BANDS)
            ]
            density = jnp.concatenate(rows, 0)
            out_ref[s] += jnp.dot(density, mixed, preferred_element_type=F32)
        return carry

    lax.fori_loop(0, 2 * SIDE, unit, 0)
    for s in range(SLOTS):
        scale = jnp.where(partners_ref[s] >= 0, 1.0 / math.sqrt(POINTS), 0.0)
        out_ref[s] = out_ref[s] * scale

    give_val.wait_send()
    give_scr.wait_send()
    for j in (1, 2, 3):
        y_step(j).wait_send()
        for h in range(2):
            sel_step(j, h).wait_send()
    z_copy.wait_send()
    cond_drain()
    mix_drain()


def on_device(screened, valence, first_band, second_band, conduction, partners):
    vmem = pl.BlockSpec(memory_space=pltpu.VMEM)
    hbm = pl.BlockSpec(memory_space=pl.ANY)
    dma = pltpu.SemaphoreType.DMA
    kernel = pl.pallas_call(
        whole_kernel,
        out_shape=jax.ShapeDtypeStruct((SLOTS, BANDS * BANDS, OWN_PAIRS), F32),
        in_specs=[pl.BlockSpec(memory_space=pltpu.SMEM), vmem, vmem, hbm, hbm, hbm],
        out_specs=vmem,
        scratch_shapes=[
            pltpu.VMEM((BANDS, POINTS), BF16),
            pltpu.VMEM((2, HALF_ROWS, 512), BF16),
            pltpu.VMEM((2, 512, 256), BF16),
            pltpu.VMEM((2, 512, PAIRS), BF16),
            pltpu.VMEM((SIDE, HALF_ROWS, OWN_PAIRS), F32),
            pltpu.VMEM((SIDE, HALF_ROWS, OWN_PAIRS), BF16),
            pltpu.VMEM((SIDE - 1, HALF_ROWS, OWN_PAIRS), BF16),
            pltpu.VMEM((HALF_ROWS, OWN_PAIRS), BF16),
            pltpu.VMEM((HALF_ROWS, OWN_PAIRS), BF16),
            pltpu.VMEM((2, SIDE, SIDE, BANDS, PIECE), BF16),
            pltpu.VMEM((2, SIDE, SIDE, HALF_ROWS, OWN_PAIRS), BF16),
            pltpu.VMEM((SIDE, 2, SLOTS * BANDS, PIECE), BF16),
            dma((4,)),
            dma((2,)),
            dma((2,)),
            dma((3,)),
            dma((3,)),
            dma,
            dma,
        ]
        + [dma((3,)), dma((3,)), dma((4,)), dma((4,)), dma((4,)), dma((4,))] * 2
        + [dma((3, 2)), dma((3, 2))],
        compiler_params=pltpu.CompilerParams(
            collective_id=0, has_side_effects=True, vmem_limit_bytes=48 * 2**20
        ),
    )(
        partners.reshape(-1),
        first_band.reshape(1, -1),
        second_band.reshape(1, -1),
        screened,
        valence,
        conduction,
    )
    return kernel.reshape((1, 1) + kernel.shape)


def solution(mesh):
    in_specs = (
        P("cond", ("grp", "val")),
        P(("grp", "val"), None),
        P(),
        P(),
        P("cond", None),
        P("grp", "cond", None),
    )
    out_specs = P("grp", "cond", None, None, "val")
    return jax.shard_map(
        on_device, mesh=mesh, in_specs=in_specs, out_specs=out_specs, check_vma=False
    )
```

time: 250 us -> 68.9 us (0.28)
  the two profiles are of different devices: /device:TPU:8 before, /device:TPU:1 now
where the time goes in v2:
time: 68.9 us; the launch traced here: 68.2 us
  Pallas kernels  61.8 us (90%)
  local copies, waits for them, and re-layouts  6.37 us (9%)
    pallas_call x1, Pallas kernels, on_device(): pl.pallas_call(whole_kernel, out_shape=jax.ShapeDtypeStruct((SLOTS, BANDS...  61.8 us
    unnamed x13, local copies, waits for them, and re-layouts  6.37 us

profile of v2, /device:TPU:1, one launch (start us, length us, event | category | flops | bytes accessed | tf_op | source)
XLA Modules:
  0.0 68.2 jit_solution(11358769185431624259)
XLA Ops:
  0.0 0.0 copy-start
  0.0 1.0 %copy-done = bf16[512,512]{1,0:T(8,128)(2,1)S(1)} copy-done((bf16[512,512]{1,0:T(8,128)(2,1)S(1)}, bf16[512,512]{1,0:T(8,128)(2,1)}, u32[]{:S(2)}) %copy-start) | copy-done | bytes 524312
  1.0 0.0 copy-start.1
  1.0 1.0 %copy-done.1 = bf16[32,8192]{1,0:T(8,128)(2,1)S(1)} copy-done((bf16[32,8192]{1,0:T(8,128)(2,1)S(1)}, bf16[32,8192]{1,0:T(8,128)(2,1)}, u32[]{:S(2)}) %copy-start.1) | copy-done | bytes 524312
  2.1 0.0 copy-start.2
  2.1 0.9 %copy-done.2 = bf16[512,256]{1,0:T(8,128)(2,1)S(1)} copy-done((bf16[512,256]{1,0:T(8,128)(2,1)S(1)}, bf16[512,256]{1,0:T(8,128)(2,1)}, u32[]{:S(2)}) %copy-start.2) | copy-done | bytes 262168
  3.0 0.0 copy-start.3
  3.0 0.7 copy-done.3
  3.7 0.0 copy-start.4
  3.7 0.7 copy-done.4
  4.4 0.0 copy-start.5
  4.4 0.7 copy-done.5
  5.1 61.8 %shard_map.64 = f32[4,1024,128]{2,1,0:T(8,128)S(1)} custom-call(s32[4]{0:T(128)S(1)} %bitcast.7, s32[1,512]{1,0:T(1,128)S(1)} %bitcast.5, s32[1,512]{1,0:T(1,128)S(1)} %bitcast.6, bf16[512,512]{1,0:T(8,128)(2,1)S(1)} %copy-done, bf16[512,256]{1,0:T(8,128)(2,1)S(1)} %copy-done.2, bf16[32,8192]{1,0:T(8,128)(2,1)S(1)} %copy-done.1), custom_call_target="tpu_custom_call" | custom-call | tf_op jit(solution)/shard_map/pallas_call | solution.py:339
  66.8 1.3 %copy.8 = f32[1,1,4,1024,128]{4,3,2,1,0:T(8,128)} copy(f32[1,1,4,1024,128]{4,3,2,1,0:T(8,128)S(1)} %bitcast.4) | data formatting | bytes 4194304
Async XLA Ops:
  0.0 1.0 %copy-start = (bf16[512,512]{1,0:T(8,128)(2,1)S(1)}, bf16[512,512]{1,0:T(8,128)(2,1)}, u32[]{:S(2)}) copy-start(bf16[512,512]{1,0:T(8,128)(2,1)} %screened_ref.1) | copy-start | bytes 1572868
  1.0 1.0 %copy-start.1 = (bf16[32,8192]{1,0:T(8,128)(2,1)S(1)}, bf16[32,8192]{1,0:T(8,128)(2,1)}, u32[]{:S(2)}) copy-start(bf16[32,8192]{1,0:T(8,128)(2,1)} %conduction_ref.1) | copy-start | bytes 1572868
  2.1 0.9 %copy-start.2 = (bf16[512,256]{1,0:T(8,128)(2,1)S(1)}, bf16[512,256]{1,0:T(8,128)(2,1)}, u32[]{:S(2)}) copy-start(bf16[512,256]{1,0:T(8,128)(2,1)} %valence_ref.1) | copy-start | bytes 786436
  3.0 0.7 %copy-start.3 = (s32[512]{0:T(512)S(1)}, s32[512]{0:T(512)}, u32[]{:S(2)}) copy-start(s32[512]{0:T(512)} %param.8) | copy-start | bytes 6148
  3.7 0.7 %copy-start.4 = (s32[512]{0:T(512)S(1)}, s32[512]{0:T(512)}, u32[]{:S(2)}) copy-start(s32[512]{0:T(512)} %param.9) | copy-start | bytes 6148
  4.4 0.7 copy-start.5

commit v3 on v1

v3 whole, which is shorter than its diff:
```python
import math

import jax
import jax.numpy as jnp
from jax import lax
from jax.experimental import pallas as pl
from jax.experimental.pallas import tpu as pltpu
from jax.sharding import PartitionSpec as P

MESH = pl.DeviceIdType.MESH
BF16 = jnp.bfloat16
F32 = jnp.float32
SIDE = 4
BANDS = 32
SLOTS = 4
POINTS = 8192
PAIRS = 512
OWN_PAIRS = 128
HALF_ROWS = 256
CHUNKS = 2
STRIP = HALF_ROWS // CHUNKS
QUARTER = POINTS // SIDE
PART = SIDE * STRIP


def whole_kernel(
    partners_ref,
    first_ref,
    second_ref,
    screened_ref,
    valence_ref,
    conduction_ref,
    out_ref,
    partners,
    bands,
    natural,
    left,
    scr,
    val,
    dens,
    pair_out,
    pair_in,
    sums,
    tosend,
    parts,
    zout,
    zin,
    gath_first,
    gath_second,
    mix,
    sel,
    sib,
    load_sem,
    pair_send,
    pair_recv,
    y_send,
    y_recv,
    z_send,
    z_recv,
    ga_send,
    ga_recv,
    gb_send,
    gb_recv,
    ma_send,
    ma_recv,
    mb_send,
    mb_recv,
    ms_send,
    ms_recv,
    own_send,
    other_send,
    near_recv,
    sib_send,
    sib_recv,
    relay_send,
    relay_recv,
):
    grp = lax.axis_index("grp")
    cond = lax.axis_index("cond")
    y = lax.axis_index("val")
    core = lax.rem(grp, 2)
    x = lax.rem(cond, SIDE)
    zlo = cond // SIDE
    z = (grp // 2) * SIDE + zlo
    par = lax.rem(x, 2)

    def device(px, py, pz, pcore):
        px = lax.rem(px + SIDE, SIDE)
        py = lax.rem(py + SIDE, SIDE)
        pz = lax.rem(pz + 2 * SIDE, 2 * SIDE)
        return ((pz // SIDE) * 2 + pcore, lax.rem(pz, SIDE) * SIDE + px, py)

    sibling = device(x, y, z, 1 - core)
    opposite = device(x, y, z + SIDE, core)

    def z_step(j, up):
        return (0, 1, up * 4 - 2, -1)[j]

    pa = x * (1 - core) + zlo * core
    pb = zlo * (1 - core) + x * core

    def peer_a(j):
        return device(x + j * (1 - core), y, z + z_step(j, par) * core, core)

    def peer_b(j, up):
        return device(x + j * core, y, z + z_step(j, up) * (1 - core), core)

    def back(p, j):
        return lax.rem(p + SIDE - j, SIDE)

    def remote(src, dst, ssem, rsem, dev):
        return pltpu.make_async_remote_copy(
            src_ref=src, dst_ref=dst, send_sem=ssem, recv_sem=rsem, device_id=dev,
            device_id_type=MESH,
        )

    copies = [
        (conduction_ref, natural),
        (first_ref, bands.at[0]),
        (second_ref, bands.at[1]),
        (valence_ref, val),
        (screened_ref, scr),
        (partners_ref, partners.at[0]),
    ]
    loads = [
        pltpu.make_async_copy(src, dst, load_sem.at[i]) for i, (src, dst) in enumerate(copies)
    ]
    load_natural, load_first, load_second, load_val, load_scr, load_partners = loads
    for load in loads:
        load.start()

    peers = [sibling, opposite]
    peers += [device(x, y + j, z, core) for j in (1, 2, 3)]
    peers += [device(x, y + j, z, 1 - core) for j in (1, 3)]
    peers += [device(x + j, y, z, core) for j in (1, 2, 3)]
    peers += [device(x, y, z + j, core) for j in (1, -1, 2, -2)]
    barrier = pltpu.get_barrier_semaphore()
    for peer in peers:
        pl.semaphore_signal(barrier, inc=1, device_id=peer, device_id_type=MESH)

    load_natural.wait()
    for q in range(SIDE):
        for t in range(CHUNKS):
            for h in range(2):
                for i in range(SIDE):
                    start = q * QUARTER + i * 2 * HALF_ROWS + h * HALF_ROWS + t * STRIP
                    left[q, t, h, :, i * STRIP : (i + 1) * STRIP] = natural[
                        :, start : start + STRIP
                    ]

    load_first.wait()
    load_second.wait()
    band = lax.broadcasted_iota(jnp.int32, (val.shape[1], PAIRS), 0)
    first_pick = jnp.where(band == bands[0], 1.0, 0.0).astype(BF16)
    second_pick = jnp.where(band == bands[1], 1.0, 0.0).astype(BF16)
    load_val.wait()
    for part in range(2):
        rows = pl.ds(part * 256, 256)
        points = val[rows, :]
        first_cols = jnp.dot(points, first_pick, preferred_element_type=F32)
        second_cols = jnp.dot(points, second_pick, preferred_element_type=F32)
        dens[rows, :] = (first_cols * second_cols).astype(BF16)
    load_scr.wait()
    for owner, kept in ((1 - core, pair_out), (core, sums)):
        for t in range(CHUNKS):
            start = pl.multiple_of(owner * HALF_ROWS + t * STRIP, STRIP)
            total = jnp.dot(scr[pl.ds(start, STRIP), :], dens[...], preferred_element_type=F32)
            for v in range(SIDE):
                kept[t, v] = total[:, v * OWN_PAIRS : (v + 1) * OWN_PAIRS]

    pl.semaphore_wait(barrier, len(peers))

    def pair_step(t):
        return remote(pair_out.at[t], pair_in.at[t], pair_send.at[t], pair_recv.at[t], sibling)

    give_partners = remote(
        partners_ref, partners.at[1], pair_send.at[CHUNKS], pair_recv.at[CHUNKS], sibling
    )
    for t in range(CHUNKS):
        pair_step(t).start()
    give_partners.start()

    low, high = pl.ds(0, 2), pl.ds(2, 2)

    class Gather:
        def __init__(self, buf, own, t, send_a, recv_a, send_b, recv_b):
            self.buf, self.own, self.t = buf, own, t
            self.send_a, self.recv_a, self.send_b, self.recv_b = send_a, recv_a, send_b, recv_b

        def step_a(self, j):
            sems = self.send_a.at[self.t, j - 1], self.recv_a.at[self.t, j - 1]
            return remote(self.own, self.buf.at[pb, pa], *sems, peer_a(j))

        def got_a(self, j):
            place = self.buf.at[pb, back(pa, j)]
            sems = self.send_a.at[self.t, j - 1], self.recv_a.at[self.t, j - 1]
            return remote(place, place, *sems, peer_a(j))

        def step_b(self, i):
            sems = self.send_b.at[self.t, i], self.recv_b.at[self.t, i]
            if i < 2:
                place = self.buf.at[pb]
                return remote(place, place, *sems, peer_b((1, 3)[i], 0))
            place = self.buf.at[pb, (low, high)[i - 2]]
            return remote(place, place, *sems, peer_b(2, i - 2))

        def got_b(self, i):
            sems = self.send_b.at[self.t, i], self.recv_b.at[self.t, i]
            if i < 2:
                place = self.buf.at[back(pb, (1, 3)[i])]
            else:
                place = self.buf.at[back(pb, 2), (low, high)[i - 2]]
            return remote(place, place, *sems, sibling)

        def start_a(self):
            for j in (1, 3, 2):
                self.step_a(j).start()

        def a_to_b(self):
            for j in (1, 3, 2):
                self.got_a(j).wait_recv()
            for i in range(4):
                self.step_b(i).start()

        def drain(self):
            for j in (1, 2, 3):
                self.step_a(j).wait_send()
            for i in range(4):
                self.step_b(i).wait_send()

    gath = (gath_first, gath_second)
    cond_gather = [
        Gather(gath[t], left.at[y, t, core], t, ga_send, ga_recv, gb_send, gb_recv)
        for t in range(CHUNKS)
    ]
    for t in range(CHUNKS):
        cond_gather[t].start_a()
        gath[t][pb, pa] = left[y, t, core]

    def y_step(j, t):
        return remote(
            tosend.at[t, lax.rem(y + j, SIDE)], parts.at[t, j - 1], y_send.at[t, j - 1],
            y_recv.at[t, j - 1], device(x, y + j, z, core),
        )

    for t in range(CHUNKS):
        pair_step(t).wait_recv()
        for v in range(SIDE):
            block = sums[t, v] + pair_in[t, v]
            sums[t, v] = block
            tosend[t, v] = block.astype(BF16)
        for j in (1, 3, 2):
            y_step(j, t).start()

    def z_copy(t):
        return remote(zout.at[t], zin.at[t], z_send.at[t], z_recv.at[t], opposite)

    for t in range(CHUNKS):
        for j in (1, 3, 2):
            y_step(j, t).wait_recv()
        summed = sums[t, y]
        for j in (1, 2, 3):
            summed += parts[t, j - 1].astype(F32)
        zout[t] = summed.astype(BF16)
        sums[t, 0] = summed
        z_copy(t).start()
    for t in range(CHUNKS):
        cond_gather[t].a_to_b()

    def own_step(j, t):
        place = sel.at[y, core, t]
        i = (j - 1) // 2
        return remote(
            place, place, own_send.at[t, i], near_recv.at[t, i, core], device(x, y + j, z, core)
        )

    def other_step(j, t):
        i = (j - 1) // 2
        return remote(
            sib.at[t], sel.at[y, core, t], other_send.at[t, i], near_recv.at[t, i, core],
            device(x, y + j, z, 1 - core),
        )

    def sib_step(t):
        return remote(sib.at[t], sel.at[y, core, t], sib_send.at[t], sib_recv.at[t], sibling)

    def near_got(j, h, t):
        place = sel.at[back(y, j), h, t]
        i = (j - 1) // 2
        return remote(place, place, own_send.at[t, i], near_recv.at[t, i, h], sibling)

    def relay_step(h, t):
        place = sel.at[back(y, (1, 3)[h]), h, t]
        return remote(
            place, place, relay_send.at[t, h], relay_recv.at[t, h],
            device(x, y + (1, 3)[h], z, core),
        )

    def relay(t):
        near_got(1, 0, t).wait_recv()
        relay_step(0, t).start()
        near_got(3, 1, t).wait_recv()
        relay_step(1, t).start()

    mix_gather = [
        Gather(mix.at[core, t], mix.at[core, t, pb, pa], t, ma_send, ma_recv, mb_send, mb_recv)
        for t in range(CHUNKS)
    ]

    def cross_step(i, t):
        place = mix.at[core, t, back(pb, (0, 1, 3, 2)[i])]
        return remote(place, place, ms_send.at[t, i], ms_recv.at[t, i], sibling)

    def cross_got(i, t):
        place = mix.at[1 - core, t, i]
        return remote(place, place, ms_send.at[t, i], ms_recv.at[t, i], sibling)

    def b_to_cross(t):
        for i in range(2):
            mix_gather[t].got_b(i).wait_recv()
            cross_step(i + 1, t).start()
        for i in range(2, 4):
            mix_gather[t].got_b(i).wait_recv()
        cross_step(3, t).start()

    def cross_all(t):
        for i in range(4):
            cross_got(i, t).wait_recv()

    for t in range(CHUNKS):
        z_copy(t).wait_recv()
        mix[core, t, pb, pa] = (sums[t, 0] + zin[t].astype(F32)).astype(BF16)
        mix_gather[t].start_a()
    load_partners.wait()
    give_partners.wait_recv()
    for t in range(CHUNKS):
        for i in range(4):
            cond_gather[t].got_b(i).wait_recv()
        for s in range(SLOTS):
            rows = pl.ds(s * BANDS, BANDS)
            for which in range(2):
                block = jnp.maximum(partners[which, s], 0)
                block_z = block // SIDE
                block_x = lax.rem(block, SIDE)
                picked = gath[t][
                    block_z * (1 - core) + block_x * core,
                    block_x * (1 - core) + block_z * core,
                ]
                if which == 0:
                    sel[y, core, t, rows, :] = picked
                else:
                    sib[t, rows, :] = picked
        for j in (1, 3):
            own_step(j, t).start()
            other_step(j, t).start()
        sib_step(t).start()

    out_ref[...] = jnp.zeros_like(out_ref)
    for t in range(CHUNKS):
        mix_gather[t].a_to_b()
        cross_step(0, t).start()
    relay(0)
    b_to_cross(0)
    cross_all(0)

    def unit(u, carry):
        t = u // SIDE
        step = lax.rem(u, SIDE)
        ahead = step + step // 2 - 2 * (step // 3)
        q = lax.rem(y + ahead, SIDE)

        def arrived(h, sem):
            place = sel.at[q, h, t]
            remote(place, place, own_send.at[0, 0], sem, sibling).wait_recv()

        @pl.when(step == 0)
        def _():
            arrived(1 - core, sib_recv.at[t])

        @pl.when(step == 1)
        def _():
            arrived(0, near_recv.at[t, 1, 0])

        @pl.when(step == 2)
        def _():
            arrived(1, near_recv.at[t, 0, 1])

        @pl.when(step == 3)
        def _():
            arrived(0, relay_recv.at[t, 0])
            arrived(1, relay_recv.at[t, 1])

        @pl.when(u == 1)
        def _():
            b_to_cross(1)

        @pl.when(u == 2)
        def _():
            relay(1)

        @pl.when(u == SIDE)
        def _():
            cross_all(1)

        mixed = jnp.concatenate(
            [mix[0, t, q, i] for i in range(SIDE)] + [mix[1, t, i, q] for i in range(SIDE)], 0
        )
        for s in range(SLOTS):
            rows = slice(s * BANDS, (s + 1) * BANDS)
            right = jnp.concatenate([sel[q, 0, t, rows, :], sel[q, 1, t, rows, :]], 1)
            blocks = []
            for i in range(BANDS):
                row = jnp.concatenate(
                    [left[q, t, 0, i : i + 1, :], left[q, t, 1, i : i + 1, :]], 1
                )
                blocks.append(jnp.broadcast_to(row, right.shape) * right)
            density = jnp.concatenate(blocks, 0)
            out_ref[s] += jnp.dot(density, mixed, preferred_element_type=F32)
        return carry

    lax.fori_loop(0, CHUNKS * SIDE, unit, 0)
    for s in range(SLOTS):
        scale = jnp.where(partners[0, s] >= 0, 1.0 / math.sqrt(POINTS), 0.0)
        out_ref[s] = out_ref[s] * scale

    give_partners.wait_send()
    for t in range(CHUNKS):
        pair_step(t).wait_send()
        for j in (1, 2, 3):
            y_step(j, t).wait_send()
        z_copy(t).wait_send()
        for j in (1, 3):
            own_step(j, t).wait_send()
            other_step(j, t).wait_send()
        sib_step(t).wait_send()
        for h in range(2):
            relay_step(h, t).wait_send()
        for i in range(4):
            cross_step(i, t).wait_send()
        cond_gather[t].drain()
        mix_gather[t].drain()


def on_device(screened, valence, first_band, second_band, conduction, partners):
    vmem = pl.BlockSpec(memory_space=pltpu.VMEM)
    hbm = pl.BlockSpec(memory_space=pltpu.HBM)
    dma = pltpu.SemaphoreType.DMA
    kernel = pl.pallas_call(
        whole_kernel,
        out_shape=jax.ShapeDtypeStruct((SLOTS, BANDS * BANDS, OWN_PAIRS), F32),
        in_specs=[hbm] * 6,
        out_specs=vmem,
        scratch_shapes=[
            pltpu.SMEM((2, SLOTS), jnp.int32),
            pltpu.VMEM((2, 1, PAIRS), jnp.int32),
            pltpu.VMEM((BANDS, POINTS), BF16),
            pltpu.VMEM((SIDE, CHUNKS, 2, BANDS, PART), BF16),
            pltpu.VMEM((2 * HALF_ROWS, 512), BF16),
            pltpu.VMEM((512, 256), BF16),
            pltpu.VMEM((512, PAIRS), BF16),
            pltpu.VMEM((CHUNKS, SIDE, STRIP, OWN_PAIRS), F32),
            pltpu.VMEM((CHUNKS, SIDE, STRIP, OWN_PAIRS), F32),
            pltpu.VMEM((CHUNKS, SIDE, STRIP, OWN_PAIRS), F32),
            pltpu.VMEM((CHUNKS, SIDE, STRIP, OWN_PAIRS), BF16),
            pltpu.VMEM((CHUNKS, SIDE - 1, STRIP, OWN_PAIRS), BF16),
            pltpu.VMEM((CHUNKS, STRIP, OWN_PAIRS), BF16),
            pltpu.VMEM((CHUNKS, STRIP, OWN_PAIRS), BF16),
            pltpu.VMEM((SIDE, SIDE, BANDS, PART), BF16),
            pltpu.VMEM((SIDE, SIDE, BANDS, PART), BF16),
            pltpu.VMEM((2, CHUNKS, SIDE, SIDE, STRIP, OWN_PAIRS), BF16),
            pltpu.VMEM((SIDE, 2, CHUNKS, SLOTS * BANDS, PART), BF16),
            pltpu.VMEM((CHUNKS, SLOTS * BANDS, PART), BF16),
            dma((6,)),
            dma((3,)),
            dma((3,)),
            dma((CHUNKS, 3)),
            dma((CHUNKS, 3)),
            dma((CHUNKS,)),
            dma((CHUNKS,)),
        ]
        + [dma((CHUNKS, 3)), dma((CHUNKS, 3)), dma((CHUNKS, 4)), dma((CHUNKS, 4))] * 2
        + [
            dma((CHUNKS, 4)),
            dma((CHUNKS, 4)),
            dma((CHUNKS, 2)),
            dma((CHUNKS, 2)),
            dma((CHUNKS, 2, 2)),
            dma((CHUNKS,)),
            dma((CHUNKS,)),
            dma((CHUNKS, 2)),
            dma((CHUNKS, 2)),
        ],
        compiler_params=pltpu.CompilerParams(
            collective_id=0, has_side_effects=True, vmem_limit_bytes=63 * 2**20
        ),
    )(
        partners.reshape(-1),
        first_band.reshape(1, -1),
        second_band.reshape(1, -1),
        screened,
        valence,
        conduction,
    )
    return kernel.reshape((1, 1) + kernel.shape)


def solution(mesh):
    in_specs = (
        P("cond", ("grp", "val")),
        P(("grp", "val"), None),
        P(),
        P(),
        P("cond", None),
        P("grp", "cond", None),
    )
    out_specs = P("grp", "cond", None, None, "val")
    return jax.shard_map(
        on_device, mesh=mesh, in_specs=in_specs, out_specs=out_specs, check_vma=False
    )
```

time: 250 us -> 62.7 us (0.25)
  the two profiles are of different devices: /device:TPU:8 before, /device:TPU:1 now
where the time goes in v3:
time: 62.7 us; the launch traced here: 62.5 us
  Pallas kernels  59.5 us (95%)
  local copies, waits for them, and re-layouts  3.05 us (5%)
    pallas_call x1, Pallas kernels, on_device(): pl.pallas_call(whole_kernel, out_shape=jax.ShapeDtypeStruct((SLOTS, BANDS...  59.5 us
    unnamed x1, local copies, waits for them, and re-layouts  3.05 us

profile of v3, /device:TPU:1, one launch (start us, length us, event | category | flops | bytes accessed | tf_op | source)
XLA Modules:
  0.0 62.5 jit_solution(6397578687099155099)
XLA Ops:
  0.0 59.5 %shard_map.64 = f32[4,1024,128]{2,1,0:T(8,128)} custom-call(s32[4]{0:T(128)} %bitcast.7, s32[1,512]{1,0:T(1,128)} %bitcast.5, s32[1,512]{1,0:T(1,128)} %bitcast.6, bf16[512,512]{1,0:T(8,128)(2,1)} %screened_ref.1, bf16[512,256]{1,0:T(8,128)(2,1)} %valence_ref.1, bf16[32,8192]{1,0:T(8,128)(2,1)} %conduction_ref.1), custom_call_target="tpu_custom_call" | custom-call | tf_op jit(solution)/shard_map/pallas_call | solution.py:448
  59.5 3.0 %copy.8 = f32[1,1,4,1024,128]{4,3,2,1,0:T(8,128)} copy(f32[1,1,4,1024,128]{4,3,2,1,0:T(8,128)} %bitcast.4) | data formatting | bytes 4194304

commit v4 on v3

--- a/solution.py
+++ b/solution.py
@@ -30,7 +30,9 @@
     screened_ref,
     valence_ref,
     conduction_ref,
+    final_ref,
     out_ref,
+    out_sem,
     partners,
     bands,
     natural,
@@ -331,9 +333,13 @@
         z_copy(t).wait_recv()
         mix[core, t, pb, pa] = (sums[t, 0] + zin[t].astype(F32)).astype(BF16)
         mix_gather[t].start_a()
+    out_ref[...] = jnp.zeros_like(out_ref)
+    for t in range(CHUNKS):
+        mix_gather[t].a_to_b()
+        cross_step(0, t).start()
     load_partners.wait()
     give_partners.wait_recv()
-    for t in range(CHUNKS):
+    def pick_and_send(t):
         for i in range(4):
             cond_gather[t].got_b(i).wait_recv()
         for s in range(SLOTS):
@@ -355,12 +361,9 @@
             other_step(j, t).start()
         sib_step(t).start()
 
-    out_ref[...] = jnp.zeros_like(out_ref)
-    for t in range(CHUNKS):
-        mix_gather[t].a_to_b()
-        cross_step(0, t).start()
-    relay(0)
+    pick_and_send(0)
     b_to_cross(0)
+    pick_and_send(1)
     cross_all(0)
 
     def unit(u, carry):
@@ -373,6 +376,15 @@
             place = sel.at[q, h, t]
             remote(place, place, own_send.at[0, 0], sem, sibling).wait_recv()
 
+        @pl.when(u == 1)
+        def _():
+            b_to_cross(1)
+            relay(0)
+
+        @pl.when(u == 3)
+        def _():
+            relay(1)
+
         @pl.when(step == 0)
         def _():
             arrived(1 - core, sib_recv.at[t])
@@ -389,14 +401,6 @@
         def _():
             arrived(0, relay_recv.at[t, 0])
             arrived(1, relay_recv.at[t, 1])
-
-        @pl.when(u == 1)
-        def _():
-            b_to_cross(1)
-
-        @pl.when(u == 2)
-        def _():
-            relay(1)
 
         @pl.when(u == SIDE)
         def _():
@@ -419,9 +423,13 @@
         return carry
 
     lax.fori_loop(0, CHUNKS * SIDE, unit, 0)
+    def write(s):
+        return pltpu.make_async_copy(out_ref.at[s], final_ref.at[s], out_sem.at[s])
+
     for s in range(SLOTS):
         scale = jnp.where(partners[0, s] >= 0, 1.0 / math.sqrt(POINTS), 0.0)
         out_ref[s] = out_ref[s] * scale
+        write(s).start()
 
     give_partners.wait_send()
     for t in range(CHUNKS):
@@ -439,6 +447,8 @@
             cross_step(i, t).wait_send()
         cond_gather[t].drain()
         mix_gather[t].drain()
+    for s in range(SLOTS):
+        write(s).wait()
 
 
 def on_device(screened, valence, first_band, second_band, conduction, partners):
@@ -449,8 +459,10 @@
         whole_kernel,
         out_shape=jax.ShapeDtypeStruct((SLOTS, BANDS * BANDS, OWN_PAIRS), F32),
         in_specs=[hbm] * 6,
-        out_specs=vmem,
+        out_specs=hbm,
         scratch_shapes=[
+            pltpu.VMEM((SLOTS, BANDS * BANDS, OWN_PAIRS), F32),
+            dma((SLOTS,)),
             pltpu.SMEM((2, SLOTS), jnp.int32),
             pltpu.VMEM((2, 1, PAIRS), jnp.int32),
             pltpu.VMEM((BANDS, POINTS), BF16),

time: 62.7 us -> 59.9 us (0.955)
  Pallas kernels: 59.5 us -> 56.7 us
    pallas_call x1, Pallas kernels: 59.5 us -> 56.7 us  [on_device(): pl.pallas_call(whole_kernel, out_shape=jax.ShapeDtypeStruct((SLOTS, BANDS...]
where the time goes in v4:
time: 59.9 us; the launch traced here: 59.8 us
  Pallas kernels  56.7 us (95%)
  local copies, waits for them, and re-layouts  3.05 us (5%)
    pallas_call x1, Pallas kernels, on_device(): pl.pallas_call(whole_kernel, out_shape=jax.ShapeDtypeStruct((SLOTS, BANDS...  56.7 us
    unnamed x1, local copies, waits for them, and re-layouts  3.05 us

profile of v4, /device:TPU:1, one launch (start us, length us, event | category | flops | bytes accessed | tf_op | source)
XLA Modules:
  0.0 59.8 jit_solution(13947214457738046754)
XLA Ops:
  0.0 56.7 %shard_map.64 = f32[4,1024,128]{2,1,0:T(8,128)} custom-call(s32[4]{0:T(128)} %bitcast.7, s32[1,512]{1,0:T(1,128)} %bitcast.5, s32[1,512]{1,0:T(1,128)} %bitcast.6, bf16[512,512]{1,0:T(8,128)(2,1)} %screened_ref.1, bf16[512,256]{1,0:T(8,128)(2,1)} %valence_ref.1, bf16[32,8192]{1,0:T(8,128)(2,1)} %conduction_ref.1), custom_call_target="tpu_custom_call" | custom-call | tf_op jit(solution)/shard_map/pallas_call | solution.py:458
  56.8 3.0 %copy.8 = f32[1,1,4,1024,128]{4,3,2,1,0:T(8,128)} copy(f32[1,1,4,1024,128]{4,3,2,1,0:T(8,128)} %bitcast.4) | data formatting | bytes 4194304

commit v5 on v4

--- a/solution.py
+++ b/solution.py
@@ -215,13 +215,13 @@
             return remote(place, place, *sems, sibling)
 
         def start_a(self):
-            for j in (1, 3, 2):
+            for j in (2, 1, 3):
                 self.step_a(j).start()
 
         def a_to_b(self):
             for j in (1, 3, 2):
                 self.got_a(j).wait_recv()
-            for i in range(4):
+            for i in (2, 3, 0, 1):
                 self.step_b(i).start()
 
         def drain(self):

time: 59.9 us -> 59 us (0.985)
  Pallas kernels: 56.7 us -> 55.4 us
    pallas_call x1, Pallas kernels: 56.7 us -> 55.4 us  [on_device(): pl.pallas_call(whole_kernel, out_shape=jax.ShapeDtypeStruct((SLOTS, BANDS...]
where the time goes in v5:
time: 59 us; the launch traced here: 58.5 us
  Pallas kernels  55.4 us (94%)
  local copies, waits for them, and re-layouts  3.05 us (5%)
    pallas_call x1, Pallas kernels, on_device(): pl.pallas_call(whole_kernel, out_shape=jax.ShapeDtypeStruct((SLOTS, BANDS...  55.4 us
    unnamed x1, local copies, waits for them, and re-layouts  3.05 us

profile of v5, /device:TPU:1, one launch (start us, length us, event | category | flops | bytes accessed | tf_op | source)
XLA Modules:
  0.0 58.5 jit_solution(4857336707657599082)
XLA Ops:
  0.0 55.4 %shard_map.64 = f32[4,1024,128]{2,1,0:T(8,128)} custom-call(s32[4]{0:T(128)} %bitcast.7, s32[1,512]{1,0:T(1,128)} %bitcast.5, s32[1,512]{1,0:T(1,128)} %bitcast.6, bf16[512,512]{1,0:T(8,128)(2,1)} %screened_ref.1, bf16[512,256]{1,0:T(8,128)(2,1)} %valence_ref.1, bf16[32,8192]{1,0:T(8,128)(2,1)} %conduction_ref.1), custom_call_target="tpu_custom_call" | custom-call | tf_op jit(solution)/shard_map/pallas_call | solution.py:458
  55.4 3.0 %copy.8 = f32[1,1,4,1024,128]{4,3,2,1,0:T(8,128)} copy(f32[1,1,4,1024,128]{4,3,2,1,0:T(8,128)} %bitcast.4) | data formatting | bytes 4194304

commit v6 on v5

--- a/solution.py
+++ b/solution.py
@@ -381,7 +381,7 @@
             b_to_cross(1)
             relay(0)
 
-        @pl.when(u == 3)
+        @pl.when(u == SIDE)
         def _():
             relay(1)
 

time: 59 us -> 59 us (level)
  no operation moved by 1% of the time
where the time goes in v6:
time: 59 us; the launch traced here: 58.5 us
  Pallas kernels  55.4 us (94%)
  local copies, waits for them, and re-layouts  3.05 us (5%)
    pallas_call x1, Pallas kernels, on_device(): pl.pallas_call(whole_kernel, out_shape=jax.ShapeDtypeStruct((SLOTS, BANDS...  55.4 us
    unnamed x1, local copies, waits for them, and re-layouts  3.05 us

profile of v6, /device:TPU:1, one launch (start us, length us, event | category | flops | bytes accessed | tf_op | source)
XLA Modules:
  0.0 58.5 jit_solution(1640167510625231443)
XLA Ops:
  0.0 55.4 %shard_map.64 = f32[4,1024,128]{2,1,0:T(8,128)} custom-call(s32[4]{0:T(128)} %bitcast.7, s32[1,512]{1,0:T(1,128)} %bitcast.5, s32[1,512]{1,0:T(1,128)} %bitcast.6, bf16[512,512]{1,0:T(8,128)(2,1)} %screened_ref.1, bf16[512,256]{1,0:T(8,128)(2,1)} %valence_ref.1, bf16[32,8192]{1,0:T(8,128)(2,1)} %conduction_ref.1), custom_call_target="tpu_custom_call" | custom-call | tf_op jit(solution)/shard_map/pallas_call | solution.py:458
  55.4 3.0 %copy.8 = f32[1,1,4,1024,128]{4,3,2,1,0:T(8,128)} copy(f32[1,1,4,1024,128]{4,3,2,1,0:T(8,128)} %bitcast.4) | data formatting | bytes 4194304
